TPU v7x, 256 devices: a whole 4x4x8 slice. The times are simulated.
256 devices in a mesh: grp: 8 (over y, core), fr: 32 (over x, z).
Axes of the slice: x: 4, y: 4, z: 8, core: 2. Of those that a mesh axis runs over, the one named last changes fastest.
Arguments:
- panel: float32 [32, 2048, 256], P('fr', 'grp'), may hold values from -2 to 2
- inverse: float32 [32, 256, 256], P('fr'), may hold values from -1 to 2, as said below
- live_rows: int32 [32], P('fr'), may hold values from 1024 to 2048, as said below
- tile_target: int32 [32, 16, 16], P('fr', 'grp'), may hold values from 0 to 255, as said below
- ancestor: float32 [8, 256, 128, 128], P('grp', 'fr'), may hold values from -6 to 6
Outputs:
- updated: float32 [8, 256, 128, 128], P('grp', 'fr')
Inputs may be any that keep to these rules, and one draw needn't show every extreme that they name: `inverse`: lower triangular for every front, diagonal entries 0.6 to 1.6. `live_rows`: at least half of 2048; some front has all 2048 rows in use. `tile_target`: an entry v of rows held by grp index g names ancestor tile v of grp row g, held by fr index v // 8; of the tiles of one device at most 3 go to any one fr index, and in every grp row one fr index receives exactly 3 from every device of that row.
All inputs are finite; a program needn't handle non-finite values.
Results may differ from a plain program's by a relative error of at most 0.0003.
Values sent between devices are 32-bit elements; how exact they have to be, the bound alone decides.
A program may use at most 64 MiB of HBM per device.

v0:
```python
import jax
import jax.numpy as jnp
from jax import lax
from jax.sharding import PartitionSpec as P


def body(panel, inverse, live_rows, tile_target, ancestor):
    row_count = panel.shape[1]
    tile_size = ancestor.shape[-1]
    owned_tiles = ancestor.shape[1]
    owners = lax.axis_size("fr")
    row_ids = lax.axis_index("grp") * row_count + lax.iota(jnp.int32, row_count)
    masked = jnp.where((row_ids < live_rows[0])[:, None], panel[0], 0.0)
    factor = lax.dot_general(
        masked,
        inverse[0],
        (((1,), (1,)), ((), ())),
        precision=lax.Precision.HIGHEST,
        preferred_element_type=jnp.float32,
    )
    schur_rows = lax.dot_general(
        factor,
        lax.all_gather(factor, "grp", axis=0, tiled=True),
        (((1,), (1,)), ((), ())),
        precision=lax.Precision.HIGHEST,
        preferred_element_type=jnp.float32,
    )
    tile_cols = schur_rows.shape[1] // tile_size
    block_rows = row_count // tile_size
    tile_total = block_rows * tile_cols
    pieces = schur_rows.reshape(block_rows, tile_size, tile_cols, tile_size).transpose(0, 2, 1, 3)
    pieces = pieces.reshape(tile_total, tile_size * tile_size)
    targets = tile_target[0].reshape(tile_total)
    capacity = 2 * tile_total // owners + 1
    owner_index = targets // owned_tiles
    onehot = (owner_index[:, None] == lax.iota(jnp.int32, owners)[None, :]).astype(jnp.int32)
    order_in = jnp.sum((jnp.cumsum(onehot, axis=0) - onehot) * onehot, axis=1)
    position = owner_index * capacity + order_in
    source = (
        jnp.zeros((owners * capacity,), jnp.int32).at[position].set(lax.iota(jnp.int32, tile_total))
    )
    filled = jnp.zeros((owners * capacity,), jnp.bool_).at[position].set(True)
    outgoing = jnp.where(filled[:, None], pieces[source], 0.0).reshape(
        owners, capacity, tile_size * tile_size
    )
    slot_values = (
        jnp.where(filled, targets[source] % owned_tiles, 0)
        .astype(jnp.float32)
        .reshape(owners, capacity)
    )
    got_tiles, got_slots = (
        lax.all_to_all(outgoing, "fr", split_axis=0, concat_axis=0, tiled=True),
        lax.all_to_all(slot_values, "fr", split_axis=0, concat_axis=0, tiled=True),
    )
    slot_index = got_slots.reshape(owners * capacity).astype(jnp.int32)
    selector = (lax.iota(jnp.int32, owned_tiles)[:, None] == slot_index[None, :]).astype(
        jnp.float32
    )
    summed = jnp.dot(
        selector,
        got_tiles.reshape(owners * capacity, tile_size * tile_size),
        precision=lax.Precision.HIGHEST,
        preferred_element_type=jnp.float32,
    )
    return (ancestor[0] - summed.reshape(owned_tiles, tile_size, tile_size))[None]


def solution(mesh):
    in_specs = (
        P("fr", "grp", None),
        P("fr", None, None),
        P("fr"),
        P("fr", "grp", None),
        P("grp", "fr", None, None),
    )
    out_specs = P("grp", "fr", None, None)
    return jax.shard_map(body, mesh=mesh, in_specs=in_specs, out_specs=out_specs, check_vma=False)
```

profile of v0, /device:TPU:101, one launch (start us, length us, event | category | flops | bytes accessed | tf_op | source)
XLA Modules:
  0.0 299.5 jit_solution(14758910215810719178)
XLA Ops:
  6.5 0.0 copy-start
  6.5 0.0 all-gather.2.cloned.1.call-start
  7.2 0.3 copy-done
  7.5 2.1 fusion.9
  9.6 0.0 all-gather.2.cloned.1.call-update
  9.6 0.8 reshape_squeeze.6
  10.4 0.8 reshape_squeeze.5
  11.1 0.1 fusion.15
  11.2 0.1 reduce_window_sum.11
  11.3 0.2 select_reduce_fusion
  11.5 0.7 scatter_custom_fusion.1
  12.2 1.2 gather_fusion
  13.4 0.7 scatter_custom_fusion
  14.1 0.7 all_to_all.9
  14.8 9.7 %all-to-all-start = ((f32[32,1,3]{2,1,0:T(1,128)}), f32[32,1,3]{2,1,0:T(1,128)S(1)}, u32[]{:S(2)}, u32[]{:S(2)}) async-start(f32[32,1,3]{2,1,0:T(1,128)} %bitcast.3), calls=%async_computation | async-start | bytes 32768 | tf_op jit(solution)/shard_map/all_to_all | solution.py:53
  24.5 0.1 broadcast_in_dim.52
  24.6 15.1 %all-gather.2.cloned.1.call-done = f32[2048,256]{1,0:T(8,128)} async-done(((f32[256,256]{1,0:T(8,128)}), f32[2048,256]{1,0:T(8,128)}) %all-gather.2.cloned.1.call-update) | async-done | bytes 2097168 | tf_op jit(solution)/shard_map/all_gather | solution.py:23
  39.7 3.6 %convolution_bitcast_fusion = f32[32,8,16,128]{3,1,2,0:T(8,128)S(1)} fusion(f32[256,256]{1,0:T(8,128)} %fusion.9, f32[2048,256]{1,0:T(8,128)} %all-gather.2.cloned.1.call-done), kind=kOutput, calls=%fused_computation.10 | convolution fusion | flops 1610612736 | bytes 4456448 | tf_op jit(solution)/shard_map/dot_general | solution.py:21
  43.4 0.4 copy.19
  43.8 0.1 bitcast_bitcast_fusion
  43.9 0.6 copy.15
  44.5 1.2 copy.31
  45.8 4.9 %gather_fusion.1 = f32[96,16384]{1,0:T(8,128)} fusion(f32[32,16384]{1,0:T(8,128)S(1)} %bitcast.51, s32[1024]{0:T(1024)S(1)} %pad_clamp_fusion), kind=kCustom, calls=%fused_computation.1 | custom fusion | bytes 12583296 | tf_op jit(solution)/shard_map/gather | solution.py:43
  50.7 7.6 %gather.10 = f32[32,3,16384]{2,1,0:T(4,128)} reshape(f32[96,16384]{1,0:T(8,128)} %gather_fusion.1) | data formatting | bytes 12582912 | tf_op jit(solution)/shard_map/gather | solution.py:43
  58.3 9.9 %broadcast_select_fusion = f32[32,3,16384]{2,1,0:T(4,128)} fusion(f32[32,3,16384]{2,1,0:T(4,128)} %gather.10, pred[32,3]{1,0:T(8,128)(4,1)S(1)} %broadcast_in_dim.52), kind=kLoop, calls=%fused_computation.7 | loop fusion | flops 1572864 | bytes 12583008 | tf_op jit(solution)/shard_map/jit(_where)/select_n | solution.py:43
  68.2 0.0 all-to-all-done
  68.2 9.4 %all-to-all-start.1 = ((f32[32,3,16384]{2,1,0:T(4,128)}), f32[32,3,16384]{2,1,0:T(4,128)}, u32[]{:S(2)}, u32[]{:S(2)}) async-start(f32[32,3,16384]{2,1,0:T(4,128)} %broadcast_select_fusion), calls=%async_computation.1 | async-start | bytes 16777216 | tf_op jit(solution)/shard_map/all_to_all | solution.py:52
  77.6 0.1 convert_reduce_fusion
  77.7 0.1 convert_element_type.20
  77.8 0.0 copy-start.1
  77.8 201.6 %all-to-all-done.1 = f32[32,3,16384]{2,1,0:T(4,128)} async-done(((f32[32,3,16384]{2,1,0:T(4,128)}), f32[32,3,16384]{2,1,0:T(4,128)}, u32[]{:S(2)}, u32[]{:S(2)}) %all-to-all-start.1) | async-done | bytes 6291488 | tf_op jit(solution)/shard_map/all_to_all | solution.py:52
  279.4 7.9 %reshape.144 = f32[96,16384]{1,0:T(8,128)} reshape(f32[32,3,16384]{2,1,0:T(4,128)} %all-to-all-done.1) | data formatting | bytes 12582912 | tf_op jit(solution)/shard_map/reshape | solution.py:61
  287.2 0.0 copy-done.1
  287.3 4.5 %fusion.6 = f32[1,8,128,128]{3,1,2,0:T(8,128)S(1)} fusion(f32[1,8,128,128]{3,2,1,0:T(8,128)S(1)} %copy-done.1, s32[96]{0:T(128)S(1)} %convert_element_type.20, f32[96,16384]{1,0:T(8,128)} %reshape.144), kind=kOutput, calls=%fused_computation.12 | convolution fusion | flops 151126784 | bytes 7340416 | tf_op jit(solution)/shard_map/dot_general | solution.py:59
  291.8 0.9 copy.17
  (8 shorter events, 0.1 us)
Async XLA Ops:
  6.5 1.0 copy-start
  6.5 33.2 %all-gather.2.cloned.1.call-start = ((), (), s32[]{:S(2)}) async-start(), calls=%async_computation.2 | async-start | bytes 2359296 | tf_op jit(solution)/shard_map/all_gather | solution.py:23
  14.8 53.4 %all-to-all-start = ((f32[32,1,3]{2,1,0:T(1,128)}), f32[32,1,3]{2,1,0:T(1,128)S(1)}, u32[]{:S(2)}, u32[]{:S(2)}) async-start(f32[32,1,3]{2,1,0:T(1,128)} %bitcast.3), calls=%async_computation | async-start | bytes 32768 | tf_op jit(solution)/shard_map/all_to_all | solution.py:53
  68.2 211.2 %all-to-all-start.1 = ((f32[32,3,16384]{2,1,0:T(4,128)}), f32[32,3,16384]{2,1,0:T(4,128)}, u32[]{:S(2)}, u32[]{:S(2)}) async-start(f32[32,3,16384]{2,1,0:T(4,128)} %broadcast_select_fusion), calls=%async_computation.1 | async-start | bytes 16777216 | tf_op jit(solution)/shard_map/all_to_all | solution.py:52
  77.8 209.5 %copy-start.1 = (f32[1,8,128,128]{3,2,1,0:T(8,128)S(1)}, f32[1,8,128,128]{3,2,1,0:T(8,128)}, u32[]{:S(2)}) copy-start(f32[1,8,128,128]{3,2,1,0:T(8,128)} %param.9) | copy-start | bytes 1572868
Sparse Core Ops, SparseCore 0:
  9.7 29.9 all-gather.1
where the time goes:
time: 300 us
  waiting for transfers between devices  217 us (72%)
  local copies, waits for them, and re-layouts  28.9 us (10%)
  starting transfers between devices  19.1 us (6%)
  between operations  14.2 us (5%)
  other arithmetic  10.4 us (3%)
  matrix products  10.2 us (3%)
    all_to_all x1, waiting for transfers between devices, body(): lax.all_to_all(outgoing, 'fr', split_axis=0, concat_axis=0, tiled=True)  202 us
    all_gather x1, waiting for transfers between devices, body(): lax.all_gather(factor, 'grp', axis=0, tiled=True)  15.1 us
    gather x2, local copies, waits for them, and re-layouts, body(): pieces[source]  12.5 us
    select_n x1, other arithmetic, body(): jnp.where(filled[:, None], pieces[source], 0.0)  9.95 us
    all_to_all x1, starting transfers between devices, body(): lax.all_to_all(slot_values, 'fr', split_axis=0, concat_axis=0, tiled=True)  9.67 us
    all_to_all x1, starting transfers between devices, body(): lax.all_to_all(outgoing, 'fr', split_axis=0, concat_axis=0, tiled=True)  9.38 us
    reshape x1, local copies, waits for them, and re-layouts, body(): got_tiles.reshape(owners * capacity, tile_size * tile_size)  7.85 us
  transfers between devices with their start and end apart: 3, of which 2 were waited for; matrix products, arithmetic and copies ran while one was open for 11% of the time, Pallas kernels for 0%

commit v1 on v0

v1 whole, which is shorter than its diff:
```python
import jax
import jax.numpy as jnp
from jax import lax
from jax.experimental import pallas as pl
from jax.experimental.pallas import tpu as pltpu
from jax.sharding import PartitionSpec as P

NX, NY, NZ = 4, 4, 8
W = 256
TILE = 128
ROWS = 256
SLOTS = 8
CHUNKS = 4
RB = TILE // CHUNKS
CAP = 3
EMPTY = SLOTS
MESH = pl.DeviceIdType.MESH
NT = (((1,), (1,)), ((), ()))


def split(x):
    high = x.astype(jnp.bfloat16)
    return high, (x - high.astype(jnp.float32)).astype(jnp.bfloat16)


def nt_dot(a, b):
    return lax.dot_general(a, b, NT, preferred_element_type=jnp.float32)


def kernel(
    live_ref, target_ref, panel_ref, inverse_ref, ancestor_ref, out_ref,
    fac, own_hi, own_lo, tiles, part, from_low, from_high, total, table, table_s,
    x_send, x_recv, t_send, t_recv, y_send, y_recv, c_send, c_recv, z_send, z_recv, local_sem,
):
    grp = lax.axis_index("grp")
    fr = lax.axis_index("fr")
    y, core = grp // 2, grp % 2
    x, z = fr // NZ, fr % NZ

    def x_dev(step):
        return (grp, ((x + step) % NX) * NZ + z)

    def y_grp(step):
        return ((y + step) % NY) * 2 + core

    def y_dev(step):
        return (y_grp(step), fr)

    def z_dev(step):
        return (grp, x * NZ + (z + step) % NZ)

    sibling = (y * 2 + (1 - core), fr)

    barrier = pltpu.get_barrier_semaphore()
    peers = [x_dev(1), x_dev(2), x_dev(3), y_dev(1), y_dev(3), sibling, z_dev(1), z_dev(7)]
    for peer in peers:
        pl.semaphore_signal(barrier, inc=1, device_id=peer, device_id_type=MESH)

    row_ids = grp * ROWS + lax.broadcasted_iota(jnp.int32, (ROWS, W), 0)
    masked = jnp.where(row_ids < live_ref[0], panel_ref[0], 0.0)
    factor = lax.dot_general(
        masked, inverse_ref[0], NT,
        precision=lax.Precision.HIGHEST, preferred_element_type=jnp.float32,
    )
    for c in range(CHUNKS):
        for half in range(2):
            at = half * TILE + c * RB
            fac[c, grp, x, half * RB : (half + 1) * RB, :] = factor[at : at + RB, :]

    lane = lax.broadcasted_iota(jnp.int32, (8, 128), 1)
    lane_owner, lane_rank = lane >> 2, lane & 3
    entries = jnp.full((8, 128), EMPTY, jnp.int32)
    count = jnp.zeros((8, 128), jnp.int32)
    for e in range(32):
        target = target_ref[0, e // 16, e % 16]
        hit = lane_owner == (target >> 3)
        entries = jnp.where(hit & (lane_rank == count), e * 16 + (target & 7), entries)
        count = count + jnp.where(hit, 1, 0)
    table[x] = entries

    pl.semaphore_wait(barrier, len(peers))
    sent = []

    def send(src, dst, send_sem, recv_sem, device):
        copy = pltpu.make_async_remote_copy(
            src_ref=src, dst_ref=dst, send_sem=send_sem, recv_sem=recv_sem,
            device_id=device, device_id_type=MESH,
        )
        copy.start()
        sent.append(copy)

    def arrived(ref, send_sem, recv_sem, device):
        pltpu.make_async_remote_copy(
            src_ref=ref, dst_ref=ref, send_sem=send_sem, recv_sem=recv_sem,
            device_id=device, device_id_type=MESH,
        ).wait_recv()

    for c in range(CHUNKS):
        mine = fac.at[c, grp, x]
        send(mine, mine, x_send.at[c, 0], x_recv.at[c, 0], x_dev(1))
        send(mine, mine, x_send.at[c, 1], x_recv.at[c, 1], x_dev(3))
        if c == 0:
            for step in range(1, NX):
                send(table.at[x], table.at[x], t_send.at[step], t_recv.at[step], x_dev(step))

    def x_forward(c):
        low, high = (x + 3) % NX, (x + 1) % NX
        piece = fac.at[c, grp, low]
        arrived(piece, x_send.at[c, 0], x_recv.at[c, 0], x_dev(1))
        half = fac.at[c, grp, low, 0:RB]
        send(half, half, x_send.at[c, 2], x_recv.at[c, 2], x_dev(1))
        piece = fac.at[c, grp, high]
        arrived(piece, x_send.at[c, 1], x_recv.at[c, 1], x_dev(3))
        half = fac.at[c, grp, high, RB : 2 * RB]
        send(half, half, x_send.at[c, 3], x_recv.at[c, 3], x_dev(3))

    def x_finish(c):
        far = (x + 2) % NX
        half = fac.at[c, grp, far, 0:RB]
        arrived(half, x_send.at[c, 2], x_recv.at[c, 2], x_dev(1))
        half = fac.at[c, grp, far, RB : 2 * RB]
        arrived(half, x_send.at[c, 3], x_recv.at[c, 3], x_dev(3))

    def y_start(c):
        blob = fac.at[c, grp]
        send(blob, blob, y_send.at[c, 0], y_recv.at[c, 0], y_dev(1))
        send(blob, blob, y_send.at[c, 1], y_recv.at[c, 1], y_dev(3))
        send(blob, blob, c_send.at[c, 0], c_recv.at[c, 0], sibling)

    def y_forward(c):
        low, high = y_grp(3), y_grp(1)
        blob = fac.at[c, low]
        arrived(blob, y_send.at[c, 0], y_recv.at[c, 0], y_dev(1))
        half = fac.at[c, low, 0:2]
        send(half, half, y_send.at[c, 2], y_recv.at[c, 2], y_dev(1))
        send(blob, blob, c_send.at[c, 1], c_recv.at[c, 1], sibling)
        blob = fac.at[c, high]
        arrived(blob, y_send.at[c, 1], y_recv.at[c, 1], y_dev(3))
        half = fac.at[c, high, 2:4]
        send(half, half, y_send.at[c, 3], y_recv.at[c, 3], y_dev(3))
        send(blob, blob, c_send.at[c, 2], c_recv.at[c, 2], sibling)

    def y_finish(c):
        far = y_grp(2)
        half = fac.at[c, far, 0:2]
        arrived(half, y_send.at[c, 2], y_recv.at[c, 2], y_dev(1))
        half = fac.at[c, far, 2:4]
        arrived(half, y_send.at[c, 3], y_recv.at[c, 3], y_dev(3))
        blob = fac.at[c, far]
        send(blob, blob, c_send.at[c, 3], c_recv.at[c, 3], sibling)

    def core_finish(c):
        for index, step in enumerate((0, 3, 1, 2)):
            blob = fac.at[c, ((y + step) % NY) * 2 + (1 - core)]
            arrived(blob, c_send.at[c, index], c_recv.at[c, index], sibling)

    def multiply(c):
        groups = ROWS // (2 * RB)

        def one(step, carry):
            front = step // (8 // groups)
            block = step % (8 // groups)
            left = fac[c, pl.ds(block * groups, groups), front].reshape(ROWS, W)
            hi, lo = split(left)
            right_hi, right_lo = own_hi[front], own_lo[front]
            res = nt_dot(hi, right_hi) + (nt_dot(hi, right_lo) + nt_dot(lo, right_hi))
            for half in range(2):
                cut = res[:, half * TILE : (half + 1) * TILE].reshape(ROWS // RB, RB, TILE)
                tiles[front, pl.ds(half * 16 + block * (ROWS // RB), ROWS // RB)] = cut
            return carry

        lax.fori_loop(0, NX * (8 // groups), one, 0)

    def combine(c):
        def one(away, carry):
            owner_z = (z + away) % NZ
            sums = [jnp.zeros((RB, TILE), jnp.float32) for _ in range(SLOTS)]
            for front in range(NX):
                for k in range(CAP):
                    entry = table_s[front, 0, (x * NZ + owner_z) * 4 + k]
                    tile = tiles[front, entry >> 4]
                    slot = jnp.full((RB, TILE), entry & 15, jnp.int32)
                    sums = [s + jnp.where(slot == i, tile, 0.0) for i, s in enumerate(sums)]
            for i in range(SLOTS):
                part[c, away, i] = sums[i]
            return carry

        lax.fori_loop(0, NZ, one, 0)

    def reduce_step(c, away):
        if away == 4:
            src = part.at[c, 4, 0:4]
            send(src, from_low.at[c, 3, 0:4], z_send.at[c, 3, 0], z_recv.at[c, 3, 0], z_dev(1))
            src = part.at[c, 4, 4:8]
            send(src, from_high.at[c, 3, 4:8], z_send.at[c, 3, 1], z_recv.at[c, 3, 1], z_dev(7))
            return
        for side, inbox, peer in ((0, from_low, z_dev(1)), (1, from_high, z_dev(7))):
            rows = slice(0, 8) if away < 3 else (slice(0, 4) if side == 0 else slice(4, 8))
            got = inbox.at[c, away, rows]
            arrived(got, z_send.at[c, away, side], z_recv.at[c, away, side], peer)
            if away == 0:
                continue
            index = away if side == 0 else NZ - away
            part[c, index, rows] = part[c, index, rows] + inbox[c, away, rows]
            send(
                part.at[c, index], inbox.at[c, away - 1],
                z_send.at[c, away - 1, side], z_recv.at[c, away - 1, side], peer,
            )
        if away == 0:
            got = part[c, 0] + (from_low[c, 0] + from_high[c, 0])
            total[:, c * RB : (c + 1) * RB, :] = got

    x_forward(0)
    for c in range(1, CHUNKS):
        x_forward(c)
    x_finish(0)
    y_start(0)
    for c in range(1, CHUNKS):
        x_finish(c)
    y_forward(0)
    if CHUNKS > 1:
        y_start(1)
    y_finish(0)
    for step in range(1, NX):
        src = table.at[(x + NX - step) % NX]
        arrived(src, t_send.at[step], t_recv.at[step], x_dev(step))
    to_scalar = pltpu.make_async_copy(table, table_s, local_sem)
    to_scalar.start()
    for c in range(CHUNKS):
        for half in range(2):
            hi, lo = split(fac[c, grp, :, half * RB : (half + 1) * RB, :])
            at = half * TILE + c * RB
            own_hi[:, at : at + RB, :] = hi
            own_lo[:, at : at + RB, :] = lo
    to_scalar.wait()

    pending = []
    for c in range(CHUNKS):
        core_finish(c)
        multiply(c)
        combine(c)
        reduce_step(c, 4)
        if c >= 1:
            reduce_step(c - 1, 2)
        if c + 1 < CHUNKS:
            y_forward(c + 1)
            if c + 2 < CHUNKS:
                y_start(c + 2)
        reduce_step(c, 3)
        if c >= 1:
            reduce_step(c - 1, 1)
        if c + 1 < CHUNKS:
            y_finish(c + 1)
        if c >= 1:
            reduce_step(c - 1, 0)
    reduce_step(CHUNKS - 1, 2)
    reduce_step(CHUNKS - 1, 1)
    reduce_step(CHUNKS - 1, 0)
    for i in range(SLOTS):
        out_ref[0, i] = ancestor_ref[0, i] - total[i].T
    for copy in sent:
        copy.wait_send()


def body(panel, inverse, live_rows, tile_target, ancestor):
    vmem = pl.BlockSpec(memory_space=pltpu.VMEM)
    smem = pl.BlockSpec(memory_space=pltpu.SMEM)
    sems = pltpu.SemaphoreType.DMA
    return pl.pallas_call(
        kernel,
        out_shape=jax.ShapeDtypeStruct(ancestor.shape, jnp.float32),
        in_specs=[smem, smem, vmem, vmem, vmem],
        out_specs=vmem,
        scratch_shapes=[
            pltpu.VMEM((CHUNKS, 8, NX, 2 * RB, W), jnp.float32),
            pltpu.VMEM((NX, ROWS, W), jnp.bfloat16),
            pltpu.VMEM((NX, ROWS, W), jnp.bfloat16),
            pltpu.VMEM((NX, 32, RB, TILE), jnp.float32),
            pltpu.VMEM((CHUNKS, NZ, SLOTS, RB, TILE), jnp.float32),
            pltpu.VMEM((CHUNKS, 4, SLOTS, RB, TILE), jnp.float32),
            pltpu.VMEM((CHUNKS, 4, SLOTS, RB, TILE), jnp.float32),
            pltpu.VMEM((SLOTS, TILE, TILE), jnp.float32),
            pltpu.VMEM((NX, 8, 128), jnp.int32),
            pltpu.SMEM((NX, 8, 128), jnp.int32),
            sems((CHUNKS, 4)), sems((CHUNKS, 4)), sems((NX,)), sems((NX,)),
            sems((CHUNKS, 4)), sems((CHUNKS, 4)), sems((CHUNKS, 4)), sems((CHUNKS, 4)),
            sems((CHUNKS, 4, 2)), sems((CHUNKS, 4, 2)), sems(()),
        ],
        compiler_params=pltpu.CompilerParams(
            collective_id=0, has_side_effects=True, vmem_limit_bytes=48 * 1024 * 1024
        ),
        cost_estimate=pl.CostEstimate(
            flops=2 * 3 * 4 * 256 * 2048 * 256, bytes_accessed=2**21, transcendentals=0
        ),
    )(live_rows, tile_target, panel, inverse, ancestor)


def solution(mesh):
    in_specs = (
        P("fr", "grp", None),
        P("fr", None, None),
        P("fr"),
        P("fr", "grp", None),
        P("grp", "fr", None, None),
    )
    out_specs = P("grp", "fr", None, None)
    return jax.shard_map(body, mesh=mesh, in_specs=in_specs, out_specs=out_specs, check_vma=False)
```

time: 300 us -> 104 us (0.35)
  the two profiles are of different devices: /device:TPU:101 before, /device:TPU:32 now
where the time goes in v1:
time: 104 us
  Pallas kernels  99.7 us (96%)
  local copies, waits for them, and re-layouts  3.74 us (4%)
    pallas_call x1, Pallas kernels, body(): pl.pallas_call(kernel, out_shape=jax.ShapeDtypeStruct(ancestor.shape, jnp...  99.7 us
    unnamed x9, local copies, waits for them, and re-layouts  3.74 us

profile of v1, /device:TPU:32, one launch (start us, length us, event | category | flops | bytes accessed | tf_op | source)
XLA Modules:
  0.0 104.1 jit_solution(1241005372712883989)
XLA Ops:
  0.0 0.0 copy-start.3
  0.7 0.0 copy-done.3
  0.7 0.0 copy-start
  0.7 1.0 copy-done
  1.7 0.0 copy-start.1
  1.7 0.9 copy-done.1
  2.7 0.0 copy-start.2
  2.7 0.9 copy-done.2
  3.6 99.7 %shard_map.55 = f32[1,8,128,128]{3,2,1,0:T(8,128)S(1)} custom-call(s32[1]{0:T(128)S(6)} %copy.7.live_ref, s32[1,2,16]{2,1,0:T(2,128)S(1)} %copy-done.3, f32[1,256,256]{2,1,0:T(8,128)S(1)} %copy-done.1, f32[1,256,256]{2,1,0:T(8,128)S(1)} %copy-done.2, f32[1,8,128,128]{3,2,1,0:T(8,128)S(1)} %copy-done), custom_call_target="tpu_custom_call" | custom-call | flops 3221225472 | bytes 2097152 | tf_op jit(solution)/shard_map/pallas_call | solution.py:269
  103.3 0.8 copy.8
Async XLA Ops:
  0.0 0.7 copy-start.3
  0.7 1.0 %copy-start = (f32[1,8,128,128]{3,2,1,0:T(8,128)S(1)}, f32[1,8,128,128]{3,2,1,0:T(8,128)}, u32[]{:S(2)}) copy-start(f32[1,8,128,128]{3,2,1,0:T(8,128)} %ancestor_ref.1) | copy-start | bytes 1572868
  1.7 0.9 copy-start.1
  2.7 0.9 copy-start.2

commit v2 on v1

--- a/solution.py
+++ b/solution.py
@@ -10,7 +10,7 @@
 TILE = 128
 ROWS = 256
 SLOTS = 8
-CHUNKS = 4
+CHUNKS = 8
 RB = TILE // CHUNKS
 CAP = 3
 EMPTY = SLOTS
@@ -28,8 +28,8 @@
 
 
 def kernel(
-    live_ref, target_ref, panel_ref, inverse_ref, ancestor_ref, out_ref,
-    fac, own_hi, own_lo, tiles, part, from_low, from_high, total, table, table_s,
+    live_ref, target_ref, panel_hbm, inverse_hbm, ancestor_hbm, out_ref,
+    panel_ref, inverse_ref, ancestor_ref, fac, own_hi, own_lo, tiles, part, from_low, from_high, total, table, table_s,
     x_send, x_recv, t_send, t_recv, y_send, y_recv, c_send, c_recv, z_send, z_recv, local_sem,
 ):
     grp = lax.axis_index("grp")
@@ -56,16 +56,14 @@
     for peer in peers:
         pl.semaphore_signal(barrier, inc=1, device_id=peer, device_id_type=MESH)
 
-    row_ids = grp * ROWS + lax.broadcasted_iota(jnp.int32, (ROWS, W), 0)
-    masked = jnp.where(row_ids < live_ref[0], panel_ref[0], 0.0)
-    factor = lax.dot_general(
-        masked, inverse_ref[0], NT,
-        precision=lax.Precision.HIGHEST, preferred_element_type=jnp.float32,
-    )
-    for c in range(CHUNKS):
-        for half in range(2):
-            at = half * TILE + c * RB
-            fac[c, grp, x, half * RB : (half + 1) * RB, :] = factor[at : at + RB, :]
+    loads = [
+        pltpu.make_async_copy(src, dst, local_sem.at[i])
+        for i, (src, dst) in enumerate(
+            ((panel_hbm.at[0], panel_ref), (inverse_hbm.at[0], inverse_ref), (ancestor_hbm.at[0], ancestor_ref))
+        )
+    ]
+    for load in loads:
+        load.start()
 
     lane = lax.broadcasted_iota(jnp.int32, (8, 128), 1)
     lane_owner, lane_rank = lane >> 2, lane & 3
@@ -76,7 +74,20 @@
         hit = lane_owner == (target >> 3)
         entries = jnp.where(hit & (lane_rank == count), e * 16 + (target & 7), entries)
         count = count + jnp.where(hit, 1, 0)
-    table[x] = entries
+    table[0] = entries
+
+    loads[0].wait()
+    loads[1].wait()
+    row_ids = grp * ROWS + lax.broadcasted_iota(jnp.int32, (ROWS, W), 0)
+    masked = jnp.where(row_ids < live_ref[0], panel_ref[...], 0.0)
+    factor = lax.dot_general(
+        masked, inverse_ref[...], NT,
+        precision=lax.Precision.HIGHEST, preferred_element_type=jnp.float32,
+    )
+    for c in range(CHUNKS):
+        for half in range(2):
+            at = half * TILE + c * RB
+            fac[c, grp, 0, half * RB : (half + 1) * RB, :] = factor[at : at + RB, :]
 
     pl.semaphore_wait(barrier, len(peers))
     sent = []
@@ -95,58 +106,51 @@
             device_id=device, device_id_type=MESH,
         ).wait_recv()
 
-    for c in range(CHUNKS):
-        mine = fac.at[c, grp, x]
-        send(mine, mine, x_send.at[c, 0], x_recv.at[c, 0], x_dev(1))
-        send(mine, mine, x_send.at[c, 1], x_recv.at[c, 1], x_dev(3))
-        if c == 0:
-            for step in range(1, NX):
-                send(table.at[x], table.at[x], t_send.at[step], t_recv.at[step], x_dev(step))
+    def x_start(c):
+        mine = fac.at[c, grp, 0]
+        send(mine, fac.at[c, grp, 3], x_send.at[c, 0], x_recv.at[c, 0], x_dev(1))
+        send(mine, fac.at[c, grp, 1], x_send.at[c, 1], x_recv.at[c, 1], x_dev(3))
 
     def x_forward(c):
-        low, high = (x + 3) % NX, (x + 1) % NX
-        piece = fac.at[c, grp, low]
-        arrived(piece, x_send.at[c, 0], x_recv.at[c, 0], x_dev(1))
-        half = fac.at[c, grp, low, 0:RB]
-        send(half, half, x_send.at[c, 2], x_recv.at[c, 2], x_dev(1))
-        piece = fac.at[c, grp, high]
-        arrived(piece, x_send.at[c, 1], x_recv.at[c, 1], x_dev(3))
-        half = fac.at[c, grp, high, RB : 2 * RB]
-        send(half, half, x_send.at[c, 3], x_recv.at[c, 3], x_dev(3))
+        low, high, far = fac.at[c, grp, 3], fac.at[c, grp, 1], fac.at[c, grp, 2]
+        arrived(low, x_send.at[c, 0], x_recv.at[c, 0], x_dev(1))
+        first = slice(0, RB)
+        send(low.at[first], far.at[first], x_send.at[c, 2], x_recv.at[c, 2], x_dev(1))
+        arrived(high, x_send.at[c, 1], x_recv.at[c, 1], x_dev(3))
+        last = slice(RB, 2 * RB)
+        send(high.at[last], far.at[last], x_send.at[c, 3], x_recv.at[c, 3], x_dev(3))
 
     def x_finish(c):
-        far = (x + 2) % NX
-        half = fac.at[c, grp, far, 0:RB]
-        arrived(half, x_send.at[c, 2], x_recv.at[c, 2], x_dev(1))
-        half = fac.at[c, grp, far, RB : 2 * RB]
-        arrived(half, x_send.at[c, 3], x_recv.at[c, 3], x_dev(3))
-
-    def y_start(c):
+        far = fac.at[c, grp, 2]
+        arrived(far.at[0:RB], x_send.at[c, 2], x_recv.at[c, 2], x_dev(1))
+        arrived(far.at[RB : 2 * RB], x_send.at[c, 3], x_recv.at[c, 3], x_dev(3))
         blob = fac.at[c, grp]
-        send(blob, blob, y_send.at[c, 0], y_recv.at[c, 0], y_dev(1))
-        send(blob, blob, y_send.at[c, 1], y_recv.at[c, 1], y_dev(3))
         send(blob, blob, c_send.at[c, 0], c_recv.at[c, 0], sibling)
+        for half in range(2):
+            hi, lo = split(fac[c, grp, :, half * RB : (half + 1) * RB, :])
+            at = half * TILE + c * RB
+            own_hi[:, at : at + RB, :] = hi
+            own_lo[:, at : at + RB, :] = lo
+
+    def y_start(c, which):
+        piece = fac.at[c, grp, 0:1] if which == 0 else fac.at[c, grp, 1:4]
+        send(piece, piece, y_send.at[c, which], y_recv.at[c, which], y_dev(1))
+        send(piece, piece, y_send.at[c, 2 + which], y_recv.at[c, 2 + which], y_dev(3))
 
     def y_forward(c):
-        low, high = y_grp(3), y_grp(1)
-        blob = fac.at[c, low]
-        arrived(blob, y_send.at[c, 0], y_recv.at[c, 0], y_dev(1))
-        half = fac.at[c, low, 0:2]
-        send(half, half, y_send.at[c, 2], y_recv.at[c, 2], y_dev(1))
-        send(blob, blob, c_send.at[c, 1], c_recv.at[c, 1], sibling)
-        blob = fac.at[c, high]
-        arrived(blob, y_send.at[c, 1], y_recv.at[c, 1], y_dev(3))
-        half = fac.at[c, high, 2:4]
-        send(half, half, y_send.at[c, 3], y_recv.at[c, 3], y_dev(3))
-        send(blob, blob, c_send.at[c, 2], c_recv.at[c, 2], sibling)
+        for side, (near, peer) in enumerate(((y_grp(3), y_dev(1)), (y_grp(1), y_dev(3)))):
+            blob = fac.at[c, near]
+            for which, piece in enumerate((blob.at[0:1], blob.at[1:4])):
+                k = 2 * side + which
+                arrived(piece, y_send.at[c, k], y_recv.at[c, k], peer)
+            half = blob.at[2 * side : 2 * side + 2]
+            send(half, half, y_send.at[c, 4 + side], y_recv.at[c, 4 + side], peer)
+            send(blob, blob, c_send.at[c, 1 + side], c_recv.at[c, 1 + side], sibling)
 
     def y_finish(c):
-        far = y_grp(2)
-        half = fac.at[c, far, 0:2]
-        arrived(half, y_send.at[c, 2], y_recv.at[c, 2], y_dev(1))
-        half = fac.at[c, far, 2:4]
-        arrived(half, y_send.at[c, 3], y_recv.at[c, 3], y_dev(3))
-        blob = fac.at[c, far]
+        blob = fac.at[c, y_grp(2)]
+        arrived(blob.at[0:2], y_send.at[c, 4], y_recv.at[c, 4], y_dev(1))
+        arrived(blob.at[2:4], y_send.at[c, 5], y_recv.at[c, 5], y_dev(3))
         send(blob, blob, c_send.at[c, 3], c_recv.at[c, 3], sibling)
 
     def core_finish(c):
@@ -210,68 +214,80 @@
             got = part[c, 0] + (from_low[c, 0] + from_high[c, 0])
             total[:, c * RB : (c + 1) * RB, :] = got
 
-    x_forward(0)
-    for c in range(1, CHUNKS):
+    for c in range(4):
+        x_start(c)
+        y_start(c, 0)
+        if c == 0:
+            for step in range(1, NX):
+                src, dst = table.at[0], table.at[NX - step]
+                send(src, dst, t_send.at[step], t_recv.at[step], x_dev(step))
+    for c in range(CHUNKS):
         x_forward(c)
-    x_finish(0)
-    y_start(0)
-    for c in range(1, CHUNKS):
+        if c + 4 < CHUNKS:
+            x_start(c + 4)
+        if c >= 2:
+            x_finish(c - 2)
+            if c < 4:
+                y_start(c - 2, 1)
+            if c == 6:
+                y_forward(0)
+                y_start(2, 1)
+                y_start(4, 0)
+    for c in range(CHUNKS - 2, CHUNKS):
         x_finish(c)
-    y_forward(0)
-    if CHUNKS > 1:
-        y_start(1)
+    y_forward(1)
+    y_start(3, 1)
+    y_start(5, 0)
+    for step in range(1, NX):
+        src = table.at[NX - step]
+        arrived(src, t_send.at[step], t_recv.at[step], x_dev(step))
+    to_scalar = pltpu.make_async_copy(table, table_s, local_sem.at[3])
+    to_scalar.start()
     y_finish(0)
-    for step in range(1, NX):
-        src = table.at[(x + NX - step) % NX]
-        arrived(src, t_send.at[step], t_recv.at[step], x_dev(step))
-    to_scalar = pltpu.make_async_copy(table, table_s, local_sem)
-    to_scalar.start()
-    for c in range(CHUNKS):
-        for half in range(2):
-            hi, lo = split(fac[c, grp, :, half * RB : (half + 1) * RB, :])
-            at = half * TILE + c * RB
-            own_hi[:, at : at + RB, :] = hi
-            own_lo[:, at : at + RB, :] = lo
     to_scalar.wait()
-
-    pending = []
-    for c in range(CHUNKS):
-        core_finish(c)
-        multiply(c)
-        combine(c)
-        reduce_step(c, 4)
-        if c >= 1:
-            reduce_step(c - 1, 2)
-        if c + 1 < CHUNKS:
-            y_forward(c + 1)
-            if c + 2 < CHUNKS:
-                y_start(c + 2)
-        reduce_step(c, 3)
-        if c >= 1:
-            reduce_step(c - 1, 1)
-        if c + 1 < CHUNKS:
-            y_finish(c + 1)
-        if c >= 1:
-            reduce_step(c - 1, 0)
-    reduce_step(CHUNKS - 1, 2)
-    reduce_step(CHUNKS - 1, 1)
-    reduce_step(CHUNKS - 1, 0)
+    for t in range(CHUNKS + 4):
+        if t < CHUNKS:
+            core_finish(t)
+            multiply(t)
+            combine(t)
+            reduce_step(t, 4)
+        if 0 <= t - 1 < CHUNKS:
+            reduce_step(t - 1, 3)
+        if t + 2 < CHUNKS:
+            y_forward(t + 2)
+            if t + 4 < CHUNKS:
+                y_start(t + 4, 1)
+            if t + 6 < CHUNKS:
+                y_start(t + 6, 0)
+        if 0 <= t - 2 < CHUNKS:
+            reduce_step(t - 2, 2)
+        if t + 1 < CHUNKS:
+            y_finish(t + 1)
+        if 0 <= t - 3 < CHUNKS:
+            reduce_step(t - 3, 1)
+        if 0 <= t - 4 < CHUNKS:
+            reduce_step(t - 4, 0)
+    loads[2].wait()
     for i in range(SLOTS):
-        out_ref[0, i] = ancestor_ref[0, i] - total[i].T
+        out_ref[0, i] = ancestor_ref[i] - total[i].T
     for copy in sent:
         copy.wait_send()
 
 
 def body(panel, inverse, live_rows, tile_target, ancestor):
     vmem = pl.BlockSpec(memory_space=pltpu.VMEM)
+    hbm = pl.BlockSpec(memory_space=pltpu.HBM)
     smem = pl.BlockSpec(memory_space=pltpu.SMEM)
     sems = pltpu.SemaphoreType.DMA
     return pl.pallas_call(
         kernel,
         out_shape=jax.ShapeDtypeStruct(ancestor.shape, jnp.float32),
-        in_specs=[smem, smem, vmem, vmem, vmem],
+        in_specs=[smem, smem, hbm, hbm, hbm],
         out_specs=vmem,
         scratch_shapes=[
+            pltpu.VMEM((ROWS, W), jnp.float32),
+            pltpu.VMEM((W, W), jnp.float32),
+            pltpu.VMEM((SLOTS, TILE, TILE), jnp.float32),
             pltpu.VMEM((CHUNKS, 8, NX, 2 * RB, W), jnp.float32),
             pltpu.VMEM((NX, ROWS, W), jnp.bfloat16),
             pltpu.VMEM((NX, ROWS, W), jnp.bfloat16),
@@ -283,11 +299,11 @@
             pltpu.VMEM((NX, 8, 128), jnp.int32),
             pltpu.SMEM((NX, 8, 128), jnp.int32),
             sems((CHUNKS, 4)), sems((CHUNKS, 4)), sems((NX,)), sems((NX,)),
-            sems((CHUNKS, 4)), sems((CHUNKS, 4)), sems((CHUNKS, 4)), sems((CHUNKS, 4)),
-            sems((CHUNKS, 4, 2)), sems((CHUNKS, 4, 2)), sems(()),
+            sems((CHUNKS, 6)), sems((CHUNKS, 6)), sems((CHUNKS, 4)), sems((CHUNKS, 4)),
+            sems((CHUNKS, 4, 2)), sems((CHUNKS, 4, 2)), sems((4,)),
         ],
         compiler_params=pltpu.CompilerParams(
-            collective_id=0, has_side_effects=True, vmem_limit_bytes=48 * 1024 * 1024
+            collective_id=0, has_side_effects=True, vmem_limit_bytes=63 * 1024 * 1024
         ),
         cost_estimate=pl.CostEstimate(
             flops=2 * 3 * 4 * 256 * 2048 * 256, bytes_accessed=2**21, transcendentals=0

time: 104 us -> 83.5 us (0.80)
  the two profiles are of different devices: /device:TPU:32 before, /device:TPU:1 now
where the time goes in v2:
time: 83.5 us; the launch traced here: 83.4 us
  Pallas kernels  80.8 us (97%)
  local copies, waits for them, and re-layouts  1.87 us (2%)
    pallas_call x1, Pallas kernels, body(): pl.pallas_call(kernel, out_shape=jax.ShapeDtypeStruct(ancestor.shape, jnp...  80.8 us
    unnamed x1, local copies, waits for them, and re-layouts  1.87 us

profile of v2, /device:TPU:1, one launch (start us, length us, event | category | flops | bytes accessed | tf_op | source)
XLA Modules:
  0.0 83.4 jit_solution(16096767985789831312)
XLA Ops:
  0.7 80.8 %shard_map.55 = f32[1,8,128,128]{3,2,1,0:T(8,128)} custom-call(s32[1]{0:T(128)S(6)} %copy.7.live_ref, s32[1,2,16]{2,1,0:T(2,128)} %target_ref.1, f32[1,256,256]{2,1,0:T(8,128)} %panel_hbm.1, f32[1,256,256]{2,1,0:T(8,128)} %inverse_hbm.1, f32[1,8,128,128]{3,2,1,0:T(8,128)} %ancestor_hbm.1), custom_call_target="tpu_custom_call" | custom-call | flops 3221225472 | bytes 2097152 | tf_op jit(solution)/shard_map/pallas_call | solution.py:282
  81.5 1.9 %copy.8 = f32[1,8,128,128]{3,2,1,0:T(8,128)} copy(f32[1,8,128,128]{3,2,1,0:T(8,128)} %shard_map.55) | data formatting | bytes 1048576

commit v3 on v2

v3 whole, which is shorter than its diff:
```python
import jax
import jax.numpy as jnp
from jax import lax
from jax.experimental import pallas as pl
from jax.experimental.pallas import tpu as pltpu
from jax.sharding import PartitionSpec as P

NX, NY, NZ = 4, 4, 8
W = 256
TILE = 128
ROWS = 256
SLOTS = 8
CHUNKS = 8
RB = TILE // CHUNKS
HALVES = ((1, slice(0, RB)), (3, slice(RB, 2 * RB)))
DIRECT = (0, 1)
ORDER = (
    ("xs", 0), ("ys", 0), ("xs", 1), ("xs", 2), ("ys", 1), ("xs", 3), ("ys", 2), ("xs", 4), ("ys", 3), ("xf", 0, 0),
    ("xf", 0, 1), ("tab",), ("xs", 5), ("xf", 1, 0), ("xf", 1, 1), ("yf", 1, 0), ("yf", 1, 1), ("xf", 2, 0),
    ("xf", 2, 1), ("xs", 6), ("xf", 3, 0), ("xf", 3, 1), ("yf", 3, 0), ("yf", 3, 1), ("xf", 4, 0), ("xf", 4, 1),
    ("xe", 0), ("ls", 0), ("xs", 7), ("xf", 5, 0), ("xf", 5, 1), ("ye", 1), ("xe", 1), ("ls", 1), ("xe", 2), ("ye", 3),
    ("xe", 3), ("xe", 4), ("xe", 5), ("ls", 2), ("lf", 0, 0), ("lf", 0, 1), ("xf", 6, 0), ("xf", 6, 1), ("xf", 7, 0),
    ("xf", 7, 1), ("lf", 1, 0), ("lf", 1, 1), ("ys", 4), ("ls", 3), ("ls", 4), ("le", 0), ("xe", 6), ("le", 1),
    ("xe", 7), ("mm", 0), ("c4", 0), ("lf", 2, 0), ("lf", 2, 1), ("cr", 0), ("mm", 1), ("c4", 1), ("cr", 1), ("ys", 5),
    ("lf", 3, 0), ("lf", 3, 1), ("ys", 6), ("lf", 4, 0), ("lf", 4, 1), ("r", 0, 3, 0), ("r", 0, 3, 1), ("le", 2),
    ("ls", 6), ("r", 1, 3, 0), ("r", 1, 3, 1), ("le", 3), ("mm", 2), ("c4", 2), ("cr", 2), ("mm", 3), ("c4", 3),
    ("le", 4), ("yf", 5, 0), ("yf", 5, 1), ("ys", 7), ("r", 0, 2, 0), ("r", 0, 2, 1), ("cr", 3), ("mm", 4), ("c4", 4),
    ("r", 1, 2, 0), ("r", 1, 2, 1), ("cr", 4), ("lf", 6, 0), ("lf", 6, 1), ("r", 2, 3, 0), ("r", 2, 3, 1), ("ye", 5),
    ("ls", 5), ("r", 3, 3, 0), ("r", 3, 3, 1), ("yf", 7, 0), ("yf", 7, 1), ("r", 0, 1, 0), ("r", 0, 1, 1),
    ("r", 4, 3, 0), ("r", 4, 3, 1), ("le", 6), ("ye", 7), ("ls", 7), ("r", 1, 1, 0), ("r", 1, 1, 1), ("lf", 5, 0),
    ("lf", 5, 1), ("r", 2, 2, 0), ("r", 2, 2, 1), ("r", 3, 2, 0), ("r", 3, 2, 1), ("r0", 0), ("lf", 7, 0), ("lf", 7, 1),
    ("le", 5), ("r", 4, 2, 0), ("r", 4, 2, 1), ("mm", 5), ("c4", 5), ("cr", 5), ("mm", 6), ("c4", 6), ("le", 7),
    ("cr", 6), ("r0", 1), ("r", 2, 1, 0), ("r", 2, 1, 1), ("mm", 7), ("c4", 7), ("r", 3, 1, 0), ("r", 3, 1, 1),
    ("cr", 7), ("r", 4, 1, 0), ("r", 4, 1, 1), ("r", 5, 3, 0), ("r", 5, 3, 1), ("r", 6, 3, 0), ("r", 6, 3, 1),
    ("r0", 2), ("r", 7, 3, 0), ("r", 7, 3, 1), ("r0", 3), ("r0", 4), ("r", 5, 2, 0), ("r", 5, 2, 1), ("r", 6, 2, 0),
    ("r", 6, 2, 1), ("r", 7, 2, 0), ("r", 7, 2, 1), ("r", 5, 1, 0), ("r", 5, 1, 1), ("r", 6, 1, 0), ("r", 6, 1, 1),
    ("r", 7, 1, 0), ("r", 7, 1, 1), ("r0", 5), ("r0", 6), ("r0", 7),
)
CAP = 3
EMPTY = SLOTS
MESH = pl.DeviceIdType.MESH
NT = (((1,), (1,)), ((), ()))


def split(x):
    high = x.astype(jnp.bfloat16)
    return high, (x - high.astype(jnp.float32)).astype(jnp.bfloat16)


def nt_dot(a, b):
    return lax.dot_general(a, b, NT, preferred_element_type=jnp.float32)


def kernel(
    live_ref, target_ref, panel_hbm, inverse_hbm, ancestor_hbm, out_ref,
    panel_ref, inverse_ref, ancestor_ref, fac, own_hi, own_lo, tiles, part, from_low, from_high, total, table, table_s,
    x_send, x_recv, t_send, t_recv, y_send, y_recv, l_send, l_recv, c_send, c_recv, z_send, z_recv, local_sem,
):
    grp = lax.axis_index("grp")
    fr = lax.axis_index("fr")
    y, core = grp // 2, grp % 2
    x, z = fr // NZ, fr % NZ

    def x_dev(step):
        return (grp, ((x + step) % NX) * NZ + z)

    def y_grp(step):
        return ((y + step) % NY) * 2 + core

    def y_dev(step):
        return (y_grp(step), fr)

    def z_dev(step):
        return (grp, x * NZ + (z + step) % NZ)

    sibling = (y * 2 + (1 - core), fr)

    barrier = pltpu.get_barrier_semaphore()
    peers = [x_dev(1), x_dev(2), x_dev(3), y_dev(1), y_dev(2), y_dev(3), sibling, z_dev(1), z_dev(7)]
    for peer in peers:
        pl.semaphore_signal(barrier, inc=1, device_id=peer, device_id_type=MESH)

    loads = [
        pltpu.make_async_copy(src, dst, local_sem.at[i])
        for i, (src, dst) in enumerate(
            ((panel_hbm.at[0], panel_ref), (inverse_hbm.at[0], inverse_ref), (ancestor_hbm.at[0], ancestor_ref))
        )
    ]
    for load in loads:
        load.start()

    lane = lax.broadcasted_iota(jnp.int32, (8, 128), 1)
    lane_owner, lane_rank = lane >> 2, lane & 3
    entries = jnp.full((8, 128), EMPTY, jnp.int32)
    count = jnp.zeros((8, 128), jnp.int32)
    for e in range(32):
        target = target_ref[0, e // 16, e % 16]
        hit = lane_owner == (target >> 3)
        entries = jnp.where(hit & (lane_rank == count), e * 16 + (target & 7), entries)
        count = count + jnp.where(hit, 1, 0)
    table[0] = entries

    loads[0].wait()
    loads[1].wait()
    row_ids = grp * ROWS + lax.broadcasted_iota(jnp.int32, (ROWS, W), 0)
    masked = jnp.where(row_ids < live_ref[0], panel_ref[...], 0.0)
    factor = lax.dot_general(
        masked, inverse_ref[...], NT,
        precision=lax.Precision.HIGHEST, preferred_element_type=jnp.float32,
    )
    for c in range(CHUNKS):
        for half in range(2):
            at = half * TILE + c * RB
            fac[c, 0, 0, 0, half * RB : (half + 1) * RB, :] = factor[at : at + RB, :]

    pl.semaphore_wait(barrier, len(peers))
    sent = []

    def send(src, dst, send_sem, recv_sem, device):
        copy = pltpu.make_async_remote_copy(
            src_ref=src, dst_ref=dst, send_sem=send_sem, recv_sem=recv_sem,
            device_id=device, device_id_type=MESH,
        )
        copy.start()
        sent.append(copy)

    def arrived(ref, send_sem, recv_sem, device):
        pltpu.make_async_remote_copy(
            src_ref=ref, dst_ref=ref, send_sem=send_sem, recv_sem=recv_sem,
            device_id=device, device_id_type=MESH,
        ).wait_recv()

    def x_start(c):
        mine = fac.at[c, 0, 0, 0]
        send(mine, fac.at[c, 0, 0, 3], x_send.at[c, 0], x_recv.at[c, 0], x_dev(1))
        send(mine, fac.at[c, 0, 0, 1], x_send.at[c, 1], x_recv.at[c, 1], x_dev(3))

    def x_forward(c, k):
        step, rows = HALVES[k]
        near, far = fac.at[c, 0, 0, NX - step], fac.at[c, 0, 0, 2]
        arrived(near, x_send.at[c, k], x_recv.at[c, k], x_dev(step))
        send(near.at[rows], far.at[rows], x_send.at[c, 2 + k], x_recv.at[c, 2 + k], x_dev(step))

    def x_finish(c):
        far = fac.at[c, 0, 0, 2]
        for k, (step, rows) in enumerate(HALVES):
            arrived(far.at[rows], x_send.at[c, 2 + k], x_recv.at[c, 2 + k], x_dev(step))
        if c % 2 == 0:
            to_sibling(c, 0)
        for half in range(2):
            hi, lo = split(fac[c, 0, 0, :, half * RB : (half + 1) * RB, :])
            at = half * TILE + c * RB
            own_hi[:, at : at + RB, :] = hi
            own_lo[:, at : at + RB, :] = lo

    def y_start(c):
        mine = fac.at[c, 0, 0, 0]
        send(mine, fac.at[c, 0, 3, 0], y_send.at[c, 0], y_recv.at[c, 0], y_dev(1))
        send(mine, fac.at[c, 0, 1, 0], y_send.at[c, 1], y_recv.at[c, 1], y_dev(3))
        if c % 2 == 0 and c in DIRECT:
            send(mine, fac.at[c, 0, 2, 0], y_send.at[c, 2], y_recv.at[c, 2], y_dev(2))

    def y_forward(c, k):
        step, rows = HALVES[k]
        near, far = fac.at[c, 0, NY - step, 0], fac.at[c, 0, 2, 0]
        arrived(near, y_send.at[c, k], y_recv.at[c, k], y_dev(step))
        send(near.at[rows], far.at[rows], y_send.at[c, 2 + k], y_recv.at[c, 2 + k], y_dev(step))

    def y_finish(c):
        far = fac.at[c, 0, 2, 0]
        for k, (step, rows) in enumerate(HALVES):
            arrived(far.at[rows], y_send.at[c, 2 + k], y_recv.at[c, 2 + k], y_dev(step))
        to_sibling(c, 0)

    def part_of(c, near):
        return fac.at[c, 0, near] if c % 2 == 0 else fac.at[c, 0, :, near]

    def to_sibling(c, near):
        there = fac.at[c, 1, near] if c % 2 == 0 else fac.at[c, 1, :, near]
        send(part_of(c, near), there, c_send.at[c, near], c_recv.at[c, near], sibling)

    def line_dev(c, step):
        return y_dev(step) if c % 2 == 0 else x_dev(step)

    def line_half(c, k):
        return slice(2 * k, 2 * k + 2) if c % 2 == 0 else (slice(1, 4), HALVES[k][1])

    def line_start(c):
        mine = part_of(c, 0).at[1:4]
        for k, step in ((0, 1), (1, 3), (2, 2)):
            if k < 2 or c in DIRECT:
                dst = part_of(c, 4 - step).at[1:4]
                send(mine, dst, l_send.at[c, k], l_recv.at[c, k], line_dev(c, step))

    def line_forward(c, k):
        step = HALVES[k][0]
        peer = line_dev(c, step)
        here = part_of(c, 4 - step)
        if c % 2 == 0:
            arrived(here.at[0:1], y_send.at[c, k], y_recv.at[c, k], peer)
        arrived(here.at[1:4], l_send.at[c, k], l_recv.at[c, k], peer)
        if c not in DIRECT:
            half = line_half(c, k)
            src, dst = here.at[half], part_of(c, 2).at[half]
            send(src, dst, l_send.at[c, 2 + k], l_recv.at[c, 2 + k], peer)
        to_sibling(c, 4 - step)

    def line_finish(c):
        here = part_of(c, 2)
        if c in DIRECT:
            if c % 2 == 0:
                arrived(here.at[0:1], y_send.at[c, 2], y_recv.at[c, 2], y_dev(2))
            arrived(here.at[1:4], l_send.at[c, 2], l_recv.at[c, 2], line_dev(c, 2))
        else:
            for k, (step, _) in enumerate(HALVES):
                arrived(here.at[line_half(c, k)], l_send.at[c, 2 + k], l_recv.at[c, 2 + k], line_dev(c, step))
        to_sibling(c, 2)

    def core_finish(c):
        for near in (0, 3, 1, 2):
            there = fac.at[c, 1, near] if c % 2 == 0 else fac.at[c, 1, :, near]
            arrived(there, c_send.at[c, near], c_recv.at[c, near], sibling)

    def multiply(c):
        core_finish(c)
        for front in range(NX):
            hi, lo = split(fac[c, :, :, front].reshape(ROWS, W))
            right_hi, right_lo = own_hi[front], own_lo[front]
            res = nt_dot(hi, right_hi) + (nt_dot(hi, right_lo) + nt_dot(lo, right_hi))
            for half in range(2):
                cut = res[:, half * TILE : (half + 1) * TILE].reshape(8, 2, RB, TILE)
                for block in range(8):
                    other = (y + block % 4) % NY * 2 + (core + block // 4) % 2
                    tiles[front, pl.ds(half * 16 + other * 2, 2)] = cut[block]

    def combine(c, first, count):
        def one(i, carry):
            away = (first + i) % NZ
            owner_z = (z + away) % NZ
            sums = [jnp.zeros((RB, TILE), jnp.float32) for _ in range(SLOTS)]
            for front in range(NX):
                for k in range(CAP):
                    entry = table_s[front, 0, (x * NZ + owner_z) * 4 + k]
                    tile = tiles[front, entry >> 4]
                    slot = jnp.full((RB, TILE), entry & 15, jnp.int32)
                    sums = [s + jnp.where(slot == i, tile, 0.0) for i, s in enumerate(sums)]
            for i in range(SLOTS):
                part[c, away, i] = sums[i]
            return carry

        lax.fori_loop(0, count, one, 0)

    def combine_far(c):
        combine(c, 4, 1)
        src = part.at[c, 4, 0:4]
        send(src, from_low.at[c, 3, 0:4], z_send.at[c, 3, 0], z_recv.at[c, 3, 0], z_dev(1))
        src = part.at[c, 4, 4:8]
        send(src, from_high.at[c, 3, 4:8], z_send.at[c, 3, 1], z_recv.at[c, 3, 1], z_dev(7))

    def combine_rest(c):
        combine(c, 5, NZ - 1)

    def reduce_step(c, away, side):
        inbox, peer = ((from_low, z_dev(1)), (from_high, z_dev(7)))[side]
        rows = slice(0, 8) if away < 3 else (slice(0, 4) if side == 0 else slice(4, 8))
        got = inbox.at[c, away, rows]
        arrived(got, z_send.at[c, away, side], z_recv.at[c, away, side], peer)
        index = away if side == 0 else NZ - away
        part[c, index, rows] = part[c, index, rows] + inbox[c, away, rows]
        send(
            part.at[c, index], inbox.at[c, away - 1],
            z_send.at[c, away - 1, side], z_recv.at[c, away - 1, side], peer,
        )

    def reduce_last(c):
        for side, inbox, peer in ((0, from_low, z_dev(1)), (1, from_high, z_dev(7))):
            arrived(inbox.at[c, 0], z_send.at[c, 0, side], z_recv.at[c, 0, side], peer)
        total[:, c * RB : (c + 1) * RB, :] = part[c, 0] + (from_low[c, 0] + from_high[c, 0])

    def table_finish():
        for step in range(1, NX):
            src = table.at[NX - step]
            arrived(src, t_send.at[step], t_recv.at[step], x_dev(step))
        to_scalar = pltpu.make_async_copy(table, table_s, local_sem.at[3])
        to_scalar.start()
        to_scalar.wait()

    for step in range(1, NX):
        send(table.at[0], table.at[NX - step], t_send.at[step], t_recv.at[step], x_dev(step))
    steps = {
        "xs": x_start, "xf": x_forward, "xe": x_finish, "ys": y_start, "yf": y_forward, "ye": y_finish,
        "ls": line_start, "lf": line_forward, "le": line_finish, "mm": multiply, "c4": combine_far,
        "cr": combine_rest, "r": reduce_step, "r0": reduce_last, "tab": table_finish,
    }
    for name, *where in ORDER:
        steps[name](*where)
    loads[2].wait()
    for i in range(SLOTS):
        out_ref[0, i] = ancestor_ref[i] - total[i].T
    for copy in sent:
        copy.wait_send()


def body(panel, inverse, live_rows, tile_target, ancestor):
    vmem = pl.BlockSpec(memory_space=pltpu.VMEM)
    hbm = pl.BlockSpec(memory_space=pltpu.HBM)
    smem = pl.BlockSpec(memory_space=pltpu.SMEM)
    sems = pltpu.SemaphoreType.DMA
    return pl.pallas_call(
        kernel,
        out_shape=jax.ShapeDtypeStruct(ancestor.shape, jnp.float32),
        in_specs=[smem, smem, hbm, hbm, hbm],
        out_specs=vmem,
        scratch_shapes=[
            pltpu.VMEM((ROWS, W), jnp.float32),
            pltpu.VMEM((W, W), jnp.float32),
            pltpu.VMEM((SLOTS, TILE, TILE), jnp.float32),
            pltpu.VMEM((CHUNKS, 2, NY, NX, 2 * RB, W), jnp.float32),
            pltpu.VMEM((NX, ROWS, W), jnp.bfloat16),
            pltpu.VMEM((NX, ROWS, W), jnp.bfloat16),
            pltpu.VMEM((NX, 32, RB, TILE), jnp.float32),
            pltpu.VMEM((CHUNKS, NZ, SLOTS, RB, TILE), jnp.float32),
            pltpu.VMEM((CHUNKS, 4, SLOTS, RB, TILE), jnp.float32),
            pltpu.VMEM((CHUNKS, 4, SLOTS, RB, TILE), jnp.float32),
            pltpu.VMEM((SLOTS, TILE, TILE), jnp.float32),
            pltpu.VMEM((NX, 8, 128), jnp.int32),
            pltpu.SMEM((NX, 8, 128), jnp.int32),
            sems((CHUNKS, 4)), sems((CHUNKS, 4)), sems((NX,)), sems((NX,)),
            sems((CHUNKS, 4)), sems((CHUNKS, 4)), sems((CHUNKS, 4)), sems((CHUNKS, 4)),
            sems((CHUNKS, 4)), sems((CHUNKS, 4)),
            sems((CHUNKS, 4, 2)), sems((CHUNKS, 4, 2)), sems((4,)),
        ],
        compiler_params=pltpu.CompilerParams(
            collective_id=0, has_side_effects=True, vmem_limit_bytes=63 * 1024 * 1024
        ),
        cost_estimate=pl.CostEstimate(
            flops=2 * 3 * 4 * 256 * 2048 * 256, bytes_accessed=2**21, transcendentals=0
        ),
    )(live_rows, tile_target, panel, inverse, ancestor)


def solution(mesh):
    in_specs = (
        P("fr", "grp", None),
        P("fr", None, None),
        P("fr"),
        P("fr", "grp", None),
        P("grp", "fr", None, None),
    )
    out_specs = P("grp", "fr", None, None)
    return jax.shard_map(body, mesh=mesh, in_specs=in_specs, out_specs=out_specs, check_vma=False)
```

time: 83.5 us -> 79.9 us (0.957)
  Pallas kernels: 80.8 us -> 77.2 us
    pallas_call x1, Pallas kernels: 80.8 us -> 77.2 us  [body(): pl.pallas_call(kernel, out_shape=jax.ShapeDtypeStruct(ancestor.shape, jnp...]
where the time goes in v3:
time: 79.9 us; the launch traced here: 79.8 us
  Pallas kernels  77.2 us (97%)
  local copies, waits for them, and re-layouts  1.87 us (2%)
    pallas_call x1, Pallas kernels, body(): pl.pallas_call(kernel, out_shape=jax.ShapeDtypeStruct(ancestor.shape, jnp...  77.2 us
    unnamed x1, local copies, waits for them, and re-layouts  1.87 us

profile of v3, /device:TPU:1, one launch (start us, length us, event | category | flops | bytes accessed | tf_op | source)
XLA Modules:
  0.0 79.8 jit_solution(8002306772299323519)
XLA Ops:
  0.7 77.2 %shard_map.55 = f32[1,8,128,128]{3,2,1,0:T(8,128)} custom-call(s32[1]{0:T(128)S(6)} %copy.7.live_ref, s32[1,2,16]{2,1,0:T(2,128)} %target_ref.1, f32[1,256,256]{2,1,0:T(8,128)} %panel_hbm.1, f32[1,256,256]{2,1,0:T(8,128)} %inverse_hbm.1, f32[1,8,128,128]{3,2,1,0:T(8,128)} %ancestor_hbm.1), custom_call_target="tpu_custom_call" | custom-call | flops 3221225472 | bytes 2097152 | tf_op jit(solution)/shard_map/pallas_call | solution.py:309
  77.9 1.9 %copy.8 = f32[1,8,128,128]{3,2,1,0:T(8,128)} copy(f32[1,8,128,128]{3,2,1,0:T(8,128)} %shard_map.55) | data formatting | bytes 1048576

commit v4 on v3

--- a/solution.py
+++ b/solution.py
@@ -13,31 +13,34 @@
 CHUNKS = 8
 RB = TILE // CHUNKS
 HALVES = ((1, slice(0, RB)), (3, slice(RB, 2 * RB)))
-DIRECT = (0, 1)
+FIRST = "xyxyxyyx"
+DIRECT_X = (0, 2)
+DIRECT = ()
 ORDER = (
-    ("xs", 0), ("ys", 0), ("xs", 1), ("xs", 2), ("ys", 1), ("xs", 3), ("ys", 2), ("xs", 4), ("ys", 3), ("xf", 0, 0),
-    ("xf", 0, 1), ("tab",), ("xs", 5), ("xf", 1, 0), ("xf", 1, 1), ("yf", 1, 0), ("yf", 1, 1), ("xf", 2, 0),
-    ("xf", 2, 1), ("xs", 6), ("xf", 3, 0), ("xf", 3, 1), ("yf", 3, 0), ("yf", 3, 1), ("xf", 4, 0), ("xf", 4, 1),
-    ("xe", 0), ("ls", 0), ("xs", 7), ("xf", 5, 0), ("xf", 5, 1), ("ye", 1), ("xe", 1), ("ls", 1), ("xe", 2), ("ye", 3),
-    ("xe", 3), ("xe", 4), ("xe", 5), ("ls", 2), ("lf", 0, 0), ("lf", 0, 1), ("xf", 6, 0), ("xf", 6, 1), ("xf", 7, 0),
-    ("xf", 7, 1), ("lf", 1, 0), ("lf", 1, 1), ("ys", 4), ("ls", 3), ("ls", 4), ("le", 0), ("xe", 6), ("le", 1),
-    ("xe", 7), ("mm", 0), ("c4", 0), ("lf", 2, 0), ("lf", 2, 1), ("cr", 0), ("mm", 1), ("c4", 1), ("cr", 1), ("ys", 5),
-    ("lf", 3, 0), ("lf", 3, 1), ("ys", 6), ("lf", 4, 0), ("lf", 4, 1), ("r", 0, 3, 0), ("r", 0, 3, 1), ("le", 2),
-    ("ls", 6), ("r", 1, 3, 0), ("r", 1, 3, 1), ("le", 3), ("mm", 2), ("c4", 2), ("cr", 2), ("mm", 3), ("c4", 3),
-    ("le", 4), ("yf", 5, 0), ("yf", 5, 1), ("ys", 7), ("r", 0, 2, 0), ("r", 0, 2, 1), ("cr", 3), ("mm", 4), ("c4", 4),
-    ("r", 1, 2, 0), ("r", 1, 2, 1), ("cr", 4), ("lf", 6, 0), ("lf", 6, 1), ("r", 2, 3, 0), ("r", 2, 3, 1), ("ye", 5),
-    ("ls", 5), ("r", 3, 3, 0), ("r", 3, 3, 1), ("yf", 7, 0), ("yf", 7, 1), ("r", 0, 1, 0), ("r", 0, 1, 1),
-    ("r", 4, 3, 0), ("r", 4, 3, 1), ("le", 6), ("ye", 7), ("ls", 7), ("r", 1, 1, 0), ("r", 1, 1, 1), ("lf", 5, 0),
-    ("lf", 5, 1), ("r", 2, 2, 0), ("r", 2, 2, 1), ("r", 3, 2, 0), ("r", 3, 2, 1), ("r0", 0), ("lf", 7, 0), ("lf", 7, 1),
-    ("le", 5), ("r", 4, 2, 0), ("r", 4, 2, 1), ("mm", 5), ("c4", 5), ("cr", 5), ("mm", 6), ("c4", 6), ("le", 7),
-    ("cr", 6), ("r0", 1), ("r", 2, 1, 0), ("r", 2, 1, 1), ("mm", 7), ("c4", 7), ("r", 3, 1, 0), ("r", 3, 1, 1),
-    ("cr", 7), ("r", 4, 1, 0), ("r", 4, 1, 1), ("r", 5, 3, 0), ("r", 5, 3, 1), ("r", 6, 3, 0), ("r", 6, 3, 1),
-    ("r0", 2), ("r", 7, 3, 0), ("r", 7, 3, 1), ("r0", 3), ("r0", 4), ("r", 5, 2, 0), ("r", 5, 2, 1), ("r", 6, 2, 0),
-    ("r", 6, 2, 1), ("r", 7, 2, 0), ("r", 7, 2, 1), ("r", 5, 1, 0), ("r", 5, 1, 1), ("r", 6, 1, 0), ("r", 6, 1, 1),
+    ("xs", 0), ("ys", 0), ("ys", 1), ("xs", 1), ("ys", 2), ("xs", 2), ("xs", 3), ("xf", 0, 0), ("xf", 0, 1), ("xs", 4),
+    ("tab",), ("yf", 1, 0), ("yf", 1, 1), ("xs", 5), ("xe", 0), ("ls", 0), ("xf", 1, 0), ("xf", 1, 1), ("xs", 6),
+    ("xf", 2, 0), ("xf", 2, 1), ("ys", 3), ("xs", 7), ("xe", 2), ("ls", 2), ("ye", 1), ("ls", 1), ("ys", 4), ("xe", 1),
+    ("xf", 3, 0), ("xf", 3, 1), ("lf", 0, 0), ("xf", 4, 0), ("xf", 4, 1), ("lf", 0, 1), ("xf", 5, 0), ("xf", 5, 1),
+    ("xf", 6, 0), ("xf", 6, 1), ("xf", 7, 0), ("xf", 7, 1), ("yf", 3, 0), ("yf", 3, 1), ("ys", 5), ("lf", 2, 0),
+    ("lf", 2, 1), ("lf", 1, 0), ("lf", 1, 1), ("xe", 3), ("xe", 4), ("ls", 4), ("xe", 5), ("xe", 6), ("le", 0),
+    ("xe", 7), ("ye", 3), ("ls", 3), ("yf", 5, 0), ("yf", 5, 1), ("mm", 0), ("le", 1), ("c4", 0), ("ys", 6), ("cr", 0),
+    ("ys", 7), ("le", 2), ("ls", 7), ("mm", 1), ("c4", 1), ("cr", 1), ("mm", 2), ("c4", 2), ("cr", 2), ("r", 0, 3, 0),
+    ("r", 0, 3, 1), ("lf", 3, 0), ("lf", 3, 1), ("lf", 4, 0), ("lf", 4, 1), ("ye", 5), ("ls", 5), ("yf", 6, 0),
+    ("yf", 6, 1), ("r", 1, 3, 0), ("r", 1, 3, 1), ("r", 2, 3, 0), ("r", 2, 3, 1), ("lf", 7, 0), ("lf", 7, 1), ("le", 3),
+    ("r", 0, 2, 0), ("r", 0, 2, 1), ("le", 4), ("mm", 3), ("c4", 3), ("r", 1, 2, 0), ("r", 1, 2, 1), ("lf", 5, 0),
+    ("lf", 5, 1), ("cr", 3), ("mm", 4), ("c4", 4), ("r", 2, 2, 0), ("r", 2, 2, 1), ("cr", 4), ("le", 7), ("ye", 6),
+    ("ls", 6), ("r", 0, 1, 0), ("r", 0, 1, 1), ("r", 3, 3, 0), ("r", 3, 3, 1), ("le", 5), ("r", 1, 1, 0),
+    ("r", 1, 1, 1), ("mm", 5), ("r", 4, 3, 0), ("r", 4, 3, 1), ("lf", 6, 0), ("lf", 6, 1), ("r", 2, 1, 0),
+    ("r", 2, 1, 1), ("r0", 0), ("c4", 5), ("cr", 5), ("le", 6), ("r", 3, 2, 0), ("r", 3, 2, 1), ("mm", 6), ("c4", 6),
+    ("cr", 6), ("mm", 7), ("c4", 7), ("r", 4, 2, 0), ("r", 4, 2, 1), ("cr", 7), ("r0", 1), ("r0", 2), ("r", 5, 3, 0),
+    ("r", 5, 3, 1), ("r", 3, 1, 0), ("r", 3, 1, 1), ("r", 6, 3, 0), ("r", 6, 3, 1), ("r", 7, 3, 0), ("r", 7, 3, 1),
+    ("r", 4, 1, 0), ("r", 4, 1, 1), ("r", 5, 2, 0), ("r", 5, 2, 1), ("r0", 3), ("r", 6, 2, 0), ("r", 6, 2, 1),
+    ("r", 7, 2, 0), ("r", 7, 2, 1), ("r0", 4), ("r", 5, 1, 0), ("r", 5, 1, 1), ("r", 6, 1, 0), ("r", 6, 1, 1),
     ("r", 7, 1, 0), ("r", 7, 1, 1), ("r0", 5), ("r0", 6), ("r0", 7),
 )
 CAP = 3
 EMPTY = SLOTS
+LATE = 20
 MESH = pl.DeviceIdType.MESH
 NT = (((1,), (1,)), ((), ()))
 
@@ -52,9 +55,9 @@
 
 
 def kernel(
-    live_ref, target_ref, panel_hbm, inverse_hbm, ancestor_hbm, out_ref,
-    panel_ref, inverse_ref, ancestor_ref, fac, own_hi, own_lo, tiles, part, from_low, from_high, total, table, table_s,
-    x_send, x_recv, t_send, t_recv, y_send, y_recv, l_send, l_recv, c_send, c_recv, z_send, z_recv, local_sem,
+    live_hbm, target_hbm, panel_hbm, inverse_hbm, ancestor_hbm, out_hbm,
+    live_ref, target_ref, out_ref, panel_ref, inverse_ref, ancestor_ref, fac, own_hi, own_lo, tiles, part, from_low, from_high, total, table, table_s,
+    x_send, x_recv, t_send, t_recv, y_send, y_recv, l_send, l_recv, c_send, c_recv, z_send, z_recv, local_sem, store_sem,
 ):
     grp = lax.axis_index("grp")
     fr = lax.axis_index("fr")
@@ -80,15 +83,15 @@
     for peer in peers:
         pl.semaphore_signal(barrier, inc=1, device_id=peer, device_id_type=MESH)
 
-    loads = [
-        pltpu.make_async_copy(src, dst, local_sem.at[i])
-        for i, (src, dst) in enumerate(
-            ((panel_hbm.at[0], panel_ref), (inverse_hbm.at[0], inverse_ref), (ancestor_hbm.at[0], ancestor_ref))
-        )
-    ]
+    pairs = (
+        (panel_hbm.at[0], panel_ref), (inverse_hbm.at[0], inverse_ref), (ancestor_hbm.at[0], ancestor_ref),
+        (target_hbm, target_ref), (live_hbm, live_ref),
+    )
+    loads = [pltpu.make_async_copy(src, dst, local_sem.at[i]) for i, (src, dst) in enumerate(pairs)]
     for load in loads:
         load.start()
 
+    loads[3].wait()
     lane = lax.broadcasted_iota(jnp.int32, (8, 128), 1)
     lane_owner, lane_rank = lane >> 2, lane & 3
     entries = jnp.full((8, 128), EMPTY, jnp.int32)
@@ -102,6 +105,7 @@
 
     loads[0].wait()
     loads[1].wait()
+    loads[4].wait()
     row_ids = grp * ROWS + lax.broadcasted_iota(jnp.int32, (ROWS, W), 0)
     masked = jnp.where(row_ids < live_ref[0], panel_ref[...], 0.0)
     factor = lax.dot_general(
@@ -134,18 +138,24 @@
         mine = fac.at[c, 0, 0, 0]
         send(mine, fac.at[c, 0, 0, 3], x_send.at[c, 0], x_recv.at[c, 0], x_dev(1))
         send(mine, fac.at[c, 0, 0, 1], x_send.at[c, 1], x_recv.at[c, 1], x_dev(3))
+        if c in DIRECT_X:
+            send(mine, fac.at[c, 0, 0, 2], x_send.at[c, 2], x_recv.at[c, 2], x_dev(2))
 
     def x_forward(c, k):
         step, rows = HALVES[k]
         near, far = fac.at[c, 0, 0, NX - step], fac.at[c, 0, 0, 2]
         arrived(near, x_send.at[c, k], x_recv.at[c, k], x_dev(step))
-        send(near.at[rows], far.at[rows], x_send.at[c, 2 + k], x_recv.at[c, 2 + k], x_dev(step))
+        if c not in DIRECT_X:
+            send(near.at[rows], far.at[rows], x_send.at[c, 2 + k], x_recv.at[c, 2 + k], x_dev(step))
 
     def x_finish(c):
         far = fac.at[c, 0, 0, 2]
-        for k, (step, rows) in enumerate(HALVES):
-            arrived(far.at[rows], x_send.at[c, 2 + k], x_recv.at[c, 2 + k], x_dev(step))
-        if c % 2 == 0:
+        if c in DIRECT_X:
+            arrived(far, x_send.at[c, 2], x_recv.at[c, 2], x_dev(2))
+        else:
+            for k, (step, rows) in enumerate(HALVES):
+                arrived(far.at[rows], x_send.at[c, 2 + k], x_recv.at[c, 2 + k], x_dev(step))
+        if FIRST[c] == "x":
             to_sibling(c, 0)
         for half in range(2):
             hi, lo = split(fac[c, 0, 0, :, half * RB : (half + 1) * RB, :])
@@ -157,7 +167,7 @@
         mine = fac.at[c, 0, 0, 0]
         send(mine, fac.at[c, 0, 3, 0], y_send.at[c, 0], y_recv.at[c, 0], y_dev(1))
         send(mine, fac.at[c, 0, 1, 0], y_send.at[c, 1], y_recv.at[c, 1], y_dev(3))
-        if c % 2 == 0 and c in DIRECT:
+        if FIRST[c] == "x" and c in DIRECT:
             send(mine, fac.at[c, 0, 2, 0], y_send.at[c, 2], y_recv.at[c, 2], y_dev(2))
 
     def y_forward(c, k):
@@ -173,17 +183,17 @@
         to_sibling(c, 0)
 
     def part_of(c, near):
-        return fac.at[c, 0, near] if c % 2 == 0 else fac.at[c, 0, :, near]
+        return fac.at[c, 0, near] if FIRST[c] == "x" else fac.at[c, 0, :, near]
 
     def to_sibling(c, near):
-        there = fac.at[c, 1, near] if c % 2 == 0 else fac.at[c, 1, :, near]
+        there = fac.at[c, 1, near] if FIRST[c] == "x" else fac.at[c, 1, :, near]
         send(part_of(c, near), there, c_send.at[c, near], c_recv.at[c, near], sibling)
 
     def line_dev(c, step):
-        return y_dev(step) if c % 2 == 0 else x_dev(step)
+        return y_dev(step) if FIRST[c] == "x" else x_dev(step)
 
     def line_half(c, k):
-        return slice(2 * k, 2 * k + 2) if c % 2 == 0 else (slice(1, 4), HALVES[k][1])
+        return slice(2 * k, 2 * k + 2) if FIRST[c] == "x" else (slice(1, 4), HALVES[k][1])
 
     def line_start(c):
         mine = part_of(c, 0).at[1:4]
@@ -196,7 +206,7 @@
         step = HALVES[k][0]
         peer = line_dev(c, step)
         here = part_of(c, 4 - step)
-        if c % 2 == 0:
+        if FIRST[c] == "x":
             arrived(here.at[0:1], y_send.at[c, k], y_recv.at[c, k], peer)
         arrived(here.at[1:4], l_send.at[c, k], l_recv.at[c, k], peer)
         if c not in DIRECT:
@@ -208,7 +218,7 @@
     def line_finish(c):
         here = part_of(c, 2)
         if c in DIRECT:
-            if c % 2 == 0:
+            if FIRST[c] == "x":
                 arrived(here.at[0:1], y_send.at[c, 2], y_recv.at[c, 2], y_dev(2))
             arrived(here.at[1:4], l_send.at[c, 2], l_recv.at[c, 2], line_dev(c, 2))
         else:
@@ -218,7 +228,7 @@
 
     def core_finish(c):
         for near in (0, 3, 1, 2):
-            there = fac.at[c, 1, near] if c % 2 == 0 else fac.at[c, 1, :, near]
+            there = fac.at[c, 1, near] if FIRST[c] == "x" else fac.at[c, 1, :, near]
             arrived(there, c_send.at[c, near], c_recv.at[c, near], sibling)
 
     def multiply(c):
@@ -281,7 +291,7 @@
         for step in range(1, NX):
             src = table.at[NX - step]
             arrived(src, t_send.at[step], t_recv.at[step], x_dev(step))
-        to_scalar = pltpu.make_async_copy(table, table_s, local_sem.at[3])
+        to_scalar = pltpu.make_async_copy(table, table_s, local_sem.at[5])
         to_scalar.start()
         to_scalar.wait()
 
@@ -292,26 +302,36 @@
         "ls": line_start, "lf": line_forward, "le": line_finish, "mm": multiply, "c4": combine_far,
         "cr": combine_rest, "r": reduce_step, "r0": reduce_last, "tab": table_finish,
     }
-    for name, *where in ORDER:
+    for index, (name, *where) in enumerate(ORDER):
+        if index == len(ORDER) - LATE:
+            for copy in sent[:-LATE]:
+                copy.wait_send()
+            del sent[:-LATE]
+            loads[2].wait()
         steps[name](*where)
-    loads[2].wait()
+    stores = []
     for i in range(SLOTS):
-        out_ref[0, i] = ancestor_ref[i] - total[i].T
+        out_ref[i] = ancestor_ref[i] - total[i].T
+        stores.append(pltpu.make_async_copy(out_ref.at[i], out_hbm.at[0, i], store_sem.at[i]))
+        stores[-1].start()
     for copy in sent:
         copy.wait_send()
+    for store in stores:
+        store.wait()
 
 
 def body(panel, inverse, live_rows, tile_target, ancestor):
-    vmem = pl.BlockSpec(memory_space=pltpu.VMEM)
     hbm = pl.BlockSpec(memory_space=pltpu.HBM)
-    smem = pl.BlockSpec(memory_space=pltpu.SMEM)
     sems = pltpu.SemaphoreType.DMA
     return pl.pallas_call(
         kernel,
         out_shape=jax.ShapeDtypeStruct(ancestor.shape, jnp.float32),
-        in_specs=[smem, smem, hbm, hbm, hbm],
-        out_specs=vmem,
+        in_specs=[hbm] * 5,
+        out_specs=hbm,
         scratch_shapes=[
+            pltpu.SMEM((1,), jnp.int32),
+            pltpu.SMEM((1, 2, 16), jnp.int32),
+            pltpu.VMEM((SLOTS, TILE, TILE), jnp.float32),
             pltpu.VMEM((ROWS, W), jnp.float32),
             pltpu.VMEM((W, W), jnp.float32),
             pltpu.VMEM((SLOTS, TILE, TILE), jnp.float32),
@@ -328,7 +348,7 @@
             sems((CHUNKS, 4)), sems((CHUNKS, 4)), sems((NX,)), sems((NX,)),
             sems((CHUNKS, 4)), sems((CHUNKS, 4)), sems((CHUNKS, 4)), sems((CHUNKS, 4)),
             sems((CHUNKS, 4)), sems((CHUNKS, 4)),
-            sems((CHUNKS, 4, 2)), sems((CHUNKS, 4, 2)), sems((4,)),
+            sems((CHUNKS, 4, 2)), sems((CHUNKS, 4, 2)), sems((6,)), sems((SLOTS,)),
         ],
         compiler_params=pltpu.CompilerParams(
             collective_id=0, has_side_effects=True, vmem_limit_bytes=63 * 1024 * 1024

time: 79.9 us -> 77.9 us (0.975)
  Pallas kernels: 77.2 us -> 75.2 us
    pallas_call x1, Pallas kernels: 77.2 us -> 75.2 us  [body(): pl.pallas_call(kernel, out_shape=jax.ShapeDtypeStruct(ancestor.shape, jnp...]
where the time goes in v4:
time: 77.9 us; the launch traced here: 77.7 us
  Pallas kernels  75.2 us (97%)
  local copies, waits for them, and re-layouts  1.87 us (2%)
    pallas_call x1, Pallas kernels, body(): pl.pallas_call(kernel, out_shape=jax.ShapeDtypeStruct(ancestor.shape, jnp...  75.2 us
    unnamed x1, local copies, waits for them, and re-layouts  1.87 us

profile of v4, /device:TPU:1, one launch (start us, length us, event | category | flops | bytes accessed | tf_op | source)
XLA Modules:
  0.0 77.7 jit_solution(1892999660120476865)
XLA Ops:
  0.7 75.2 %shard_map.55 = f32[1,8,128,128]{3,2,1,0:T(8,128)} custom-call(s32[1]{0:T(128)S(6)} %copy.7.live_hbm, s32[1,2,16]{2,1,0:T(2,128)} %target_hbm.1, f32[1,256,256]{2,1,0:T(8,128)} %panel_hbm.1, f32[1,256,256]{2,1,0:T(8,128)} %inverse_hbm.1, f32[1,8,128,128]{3,2,1,0:T(8,128)} %ancestor_hbm.1), custom_call_target="tpu_custom_call" | custom-call | flops 3221225472 | bytes 2097152 | tf_op jit(solution)/shard_map/pallas_call | solution.py:326
  75.9 1.9 %copy.8 = f32[1,8,128,128]{3,2,1,0:T(8,128)} copy(f32[1,8,128,128]{3,2,1,0:T(8,128)} %shard_map.55) | data formatting | bytes 1048576

commit v5 on v4

--- a/solution.py
+++ b/solution.py
@@ -23,16 +23,16 @@
     ("xf", 3, 0), ("xf", 3, 1), ("lf", 0, 0), ("xf", 4, 0), ("xf", 4, 1), ("lf", 0, 1), ("xf", 5, 0), ("xf", 5, 1),
     ("xf", 6, 0), ("xf", 6, 1), ("xf", 7, 0), ("xf", 7, 1), ("yf", 3, 0), ("yf", 3, 1), ("ys", 5), ("lf", 2, 0),
     ("lf", 2, 1), ("lf", 1, 0), ("lf", 1, 1), ("xe", 3), ("xe", 4), ("ls", 4), ("xe", 5), ("xe", 6), ("le", 0),
-    ("xe", 7), ("ye", 3), ("ls", 3), ("yf", 5, 0), ("yf", 5, 1), ("mm", 0), ("le", 1), ("c4", 0), ("ys", 6), ("cr", 0),
+    ("xe", 7), ("mm", 0), ("c4", 0), ("ye", 3), ("ls", 3), ("yf", 5, 0), ("yf", 5, 1), ("le", 1), ("ys", 6), ("cr", 0),
     ("ys", 7), ("le", 2), ("ls", 7), ("mm", 1), ("c4", 1), ("cr", 1), ("mm", 2), ("c4", 2), ("cr", 2), ("r", 0, 3, 0),
     ("r", 0, 3, 1), ("lf", 3, 0), ("lf", 3, 1), ("lf", 4, 0), ("lf", 4, 1), ("ye", 5), ("ls", 5), ("yf", 6, 0),
     ("yf", 6, 1), ("r", 1, 3, 0), ("r", 1, 3, 1), ("r", 2, 3, 0), ("r", 2, 3, 1), ("lf", 7, 0), ("lf", 7, 1), ("le", 3),
     ("r", 0, 2, 0), ("r", 0, 2, 1), ("le", 4), ("mm", 3), ("c4", 3), ("r", 1, 2, 0), ("r", 1, 2, 1), ("lf", 5, 0),
     ("lf", 5, 1), ("cr", 3), ("mm", 4), ("c4", 4), ("r", 2, 2, 0), ("r", 2, 2, 1), ("cr", 4), ("le", 7), ("ye", 6),
     ("ls", 6), ("r", 0, 1, 0), ("r", 0, 1, 1), ("r", 3, 3, 0), ("r", 3, 3, 1), ("le", 5), ("r", 1, 1, 0),
-    ("r", 1, 1, 1), ("mm", 5), ("r", 4, 3, 0), ("r", 4, 3, 1), ("lf", 6, 0), ("lf", 6, 1), ("r", 2, 1, 0),
-    ("r", 2, 1, 1), ("r0", 0), ("c4", 5), ("cr", 5), ("le", 6), ("r", 3, 2, 0), ("r", 3, 2, 1), ("mm", 6), ("c4", 6),
-    ("cr", 6), ("mm", 7), ("c4", 7), ("r", 4, 2, 0), ("r", 4, 2, 1), ("cr", 7), ("r0", 1), ("r0", 2), ("r", 5, 3, 0),
+    ("r", 1, 1, 1), ("mm", 5), ("c4", 5), ("r", 4, 3, 0), ("r", 4, 3, 1), ("lf", 6, 0), ("lf", 6, 1), ("r", 2, 1, 0),
+    ("r", 2, 1, 1), ("r0", 0), ("cr", 5), ("le", 6), ("r", 3, 2, 0), ("r", 3, 2, 1), ("mm", 6), ("c4", 6), ("cr", 6),
+    ("mm", 7), ("c4", 7), ("r", 4, 2, 0), ("r", 4, 2, 1), ("cr", 7), ("r0", 1), ("r0", 2), ("r", 5, 3, 0),
     ("r", 5, 3, 1), ("r", 3, 1, 0), ("r", 3, 1, 1), ("r", 6, 3, 0), ("r", 6, 3, 1), ("r", 7, 3, 0), ("r", 7, 3, 1),
     ("r", 4, 1, 0), ("r", 4, 1, 1), ("r", 5, 2, 0), ("r", 5, 2, 1), ("r0", 3), ("r", 6, 2, 0), ("r", 6, 2, 1),
     ("r", 7, 2, 0), ("r", 7, 2, 1), ("r0", 4), ("r", 5, 1, 0), ("r", 5, 1, 1), ("r", 6, 1, 0), ("r", 6, 1, 1),

time: 77.9 us -> 77.9 us (level)
  no operation moved by 1% of the time
where the time goes in v5:
time: 77.9 us; the launch traced here: 77.8 us
  Pallas kernels  75.2 us (97%)
  local copies, waits for them, and re-layouts  1.87 us (2%)
    pallas_call x1, Pallas kernels, body(): pl.pallas_call(kernel, out_shape=jax.ShapeDtypeStruct(ancestor.shape, jnp...  75.2 us
    unnamed x1, local copies, waits for them, and re-layouts  1.87 us

profile of v5, /device:TPU:1, one launch (start us, length us, event | category | flops | bytes accessed | tf_op | source)
XLA Modules:
  0.0 77.8 jit_solution(13865322418664023079)
XLA Ops:
  0.7 75.2 %shard_map.55 = f32[1,8,128,128]{3,2,1,0:T(8,128)} custom-call(s32[1]{0:T(128)S(6)} %copy.7.live_hbm, s32[1,2,16]{2,1,0:T(2,128)} %target_hbm.1, f32[1,256,256]{2,1,0:T(8,128)} %panel_hbm.1, f32[1,256,256]{2,1,0:T(8,128)} %inverse_hbm.1, f32[1,8,128,128]{3,2,1,0:T(8,128)} %ancestor_hbm.1), custom_call_target="tpu_custom_call" | custom-call | flops 3221225472 | bytes 2097152 | tf_op jit(solution)/shard_map/pallas_call | solution.py:326
  75.9 1.9 %copy.8 = f32[1,8,128,128]{3,2,1,0:T(8,128)} copy(f32[1,8,128,128]{3,2,1,0:T(8,128)} %shard_map.55) | data formatting | bytes 1048576
